TPU v7x, 32 devices: a whole 2x2x4 slice. The times are simulated.
32 devices in a mesh: dp: 4 (over x, core), expert: 8 (over z, y).
Axes of the slice: x: 2, y: 2, z: 4, core: 2. Of those that a mesh axis runs over, the one named last changes fastest.
Arguments:
- tokens: bfloat16 [1024, 2048], P('expert', 'dp'), may hold values from -6 to 6
- cotangent: bfloat16 [1024, 2048], P('expert', 'dp'), may hold values from -6 to 6
- route: int32 [1024, 8], P('expert'), may hold values from 0 to 23, all different within a row; in each aligned block of 128 rows (0 to 127, 128 to 255, ...) at most 44 rows name the same one
- gate_prob: float32 [1024, 8], P('expert'), may hold values from 0.02 to 0.25
- replica_pick: int32 [8], replicated, may hold values from 0 to 1
- w_gate: bfloat16 [16, 1536, 2048], P('expert', 'dp'), may hold values from -0.125 to 0.125
- w_up: bfloat16 [16, 1536, 2048], P('expert', 'dp'), may hold values from -0.125 to 0.125
- w_down: bfloat16 [16, 1536, 2048], P('expert', 'dp'), may hold values from -0.15625 to 0.15625
Outputs:
- layer_out: bfloat16 [1024, 2048], P('expert', 'dp')
- token_grad: bfloat16 [1024, 2048], P('expert', 'dp')
- gate_grad: float32 [1024, 8], P('expert', 'dp')
- w_gate_grad: bfloat16 [16, 1536, 2048], P('expert', 'dp')
- w_up_grad: bfloat16 [16, 1536, 2048], P('expert', 'dp')
- w_down_grad: bfloat16 [16, 1536, 2048], P('expert', 'dp')
Inputs may be any that keep to these rules, and one draw needn't show every extreme that they name: `route`: each row names 8 different copies. Among the rows of one device, in aligned blocks of 128 tokens, no copy is named more than 44 times, a bound that some block reaches.
All inputs are finite; a program needn't handle non-finite values.
Results may differ from a plain program's by a relative error of at most 0.014.
Values may be sent and summed in bfloat16 or wider, within the bound.
A program may use at most 128 MiB of HBM per device.

v0:
```python
import jax
import jax.numpy as jnp
from jax import lax
from jax.sharding import PartitionSpec as P


def expert_math(rows_in, rows_cot, wide_w, down_w):
    width = down_w.shape[1]
    both = jnp.einsum("cmd,cfd->cmf", rows_in, wide_w, preferred_element_type=jnp.float32)
    gate_act = both[..., :width]
    up_act = both[..., width:]
    sigmoid_gate = jax.nn.sigmoid(gate_act)
    activated = gate_act * sigmoid_gate
    hidden = (activated * up_act).astype(jnp.bfloat16)
    out_rows = jnp.einsum("cmf,cfd->cmd", hidden, down_w, preferred_element_type=jnp.float32)
    d_hidden = jnp.einsum("cmd,cfd->cmf", rows_cot, down_w, preferred_element_type=jnp.float32)
    d_gate = (d_hidden * up_act * sigmoid_gate * (1.0 + gate_act * (1.0 - sigmoid_gate))).astype(
        jnp.bfloat16
    )
    d_up = (d_hidden * activated).astype(jnp.bfloat16)
    d_both = jnp.concatenate([d_gate, d_up], axis=2)
    back_rows = jnp.einsum("cmf,cfd->cmd", d_both, wide_w, preferred_element_type=jnp.float32)
    grad_wide = jnp.einsum("cmf,cmd->cfd", d_both, rows_in, preferred_element_type=jnp.float32)
    grad_down = jnp.einsum("cmf,cmd->cfd", hidden, rows_cot, preferred_element_type=jnp.float32)
    return (out_rows, back_rows, grad_wide, grad_down)


def regroup(values, owned, guest_shift):
    return jnp.concatenate(
        [values[:, :owned], jnp.roll(values[:, owned:], guest_shift, axis=0)], axis=1
    )


def body(tokens, cotangent, route, gate_prob, replica_pick, w_gate, w_up, w_down):
    groups = lax.axis_size("expert")
    column = lax.axis_index("expert")
    tok_dev, slice_width = tokens.shape
    fanout = route.shape[1]
    owned, width, features = w_gate.shape
    local_copies = owned + 1
    copies = groups * local_copies
    capacity = tok_dev * fanout // copies + 2
    half_axis = groups // 2
    choice_count = tok_dev * fanout
    route_rows = route.reshape(-1)
    onehot = (route_rows[:, None] == jnp.arange(copies, dtype=jnp.int32)[None, :]).astype(jnp.int32)
    position = jnp.sum((jnp.cumsum(onehot, axis=0) - 1) * onehot, axis=1)
    address = route_rows * capacity + position
    slot_source = (
        jnp.full((copies * capacity,), choice_count, jnp.int32)
        .at[address]
        .set(jnp.arange(choice_count, dtype=jnp.int32))
    )
    slot_token = slot_source // fanout
    slot_gate = jnp.concatenate([gate_prob.reshape(-1), jnp.zeros((1,), jnp.float32)], axis=0)[
        slot_source
    ]
    span = tokens.shape[1]
    pad_tok = jnp.concatenate([tokens, jnp.zeros((1, span), jnp.bfloat16)], axis=0)
    pad_cot = jnp.concatenate([cotangent, jnp.zeros((1, span), jnp.bfloat16)], axis=0)
    send_in = pad_tok[slot_token].reshape(groups, local_copies, capacity, span)
    send_cot = (slot_gate[:, None] * pad_cot[slot_token].astype(jnp.float32)).astype(jnp.bfloat16)
    send_cot = send_cot.reshape(groups, local_copies, capacity, span)
    send_in, send_cot = (regroup(send_in, owned, half_axis), regroup(send_cot, owned, half_axis))
    thin_in, thin_cot = (
        lax.all_to_all(send_in, "expert", split_axis=0, concat_axis=2, tiled=True),
        lax.all_to_all(send_cot, "expert", split_axis=0, concat_axis=2, tiled=True),
    )
    recv_in, recv_cot = (
        lax.all_gather(thin_in, "dp", axis=3, tiled=True),
        lax.all_gather(thin_cot, "dp", axis=3, tiled=True),
    )
    recv_in = recv_in[0]
    recv_cot = recv_cot[0]
    partner = (column + half_axis) % groups
    own_pick = replica_pick[partner]
    select = (jnp.arange(owned, dtype=jnp.int32) == own_pick).astype(jnp.float32)[:, None, None]
    chosen_gate = lax.dynamic_index_in_dim(w_gate, own_pick, 0, keepdims=False)
    chosen_up = lax.dynamic_index_in_dim(w_up, own_pick, 0, keepdims=False)
    chosen_down = lax.dynamic_index_in_dim(w_down, own_pick, 0, keepdims=False)
    wide_own = jnp.concatenate([w_gate, w_up], axis=1)
    wide_all = jnp.concatenate(
        [wide_own, jnp.concatenate([chosen_gate, chosen_up], axis=0)[None]], axis=0
    )
    down_all = jnp.concatenate([w_down, chosen_down[None]], axis=0)
    out_rows, back_rows, grad_wide, grad_down = expert_math(recv_in, recv_cot, wide_all, down_all)
    own_wide = grad_wide[:owned]
    own_down = grad_down[:owned]
    extra_wide = grad_wide[owned]
    extra_down = grad_down[owned]
    w_gate_grad = (own_wide[:, :width] + select * extra_wide[:width]).astype(jnp.bfloat16)
    w_up_grad = (own_wide[:, width:] + select * extra_wide[width:]).astype(jnp.bfloat16)
    w_down_grad = (own_down + select * extra_down).astype(jnp.bfloat16)
    summed_out, summed_back = (
        lax.psum_scatter(
            out_rows.astype(jnp.bfloat16), "dp", scatter_dimension=2, tiled=True
        ).astype(jnp.float32),
        lax.psum_scatter(
            back_rows.astype(jnp.bfloat16), "dp", scatter_dimension=2, tiled=True
        ).astype(jnp.float32),
    )
    got_out, got_back = (
        lax.all_to_all(
            summed_out[None].astype(jnp.bfloat16), "expert", split_axis=2, concat_axis=0, tiled=True
        ).astype(jnp.float32),
        lax.all_to_all(
            summed_back[None].astype(jnp.bfloat16),
            "expert",
            split_axis=2,
            concat_axis=0,
            tiled=True,
        ).astype(jnp.float32),
    )
    got_out = regroup(got_out, owned, half_axis)
    got_back = regroup(got_back, owned, half_axis)
    expert_slice = got_out.reshape(copies * capacity, slice_width)[address].reshape(
        tok_dev, fanout, slice_width
    )
    picked_back = got_back.reshape(copies * capacity, slice_width)[address].reshape(
        tok_dev, fanout, slice_width
    )
    token_grad = jnp.sum(picked_back, axis=1)
    layer_out = jnp.sum(gate_prob[:, :, None] * expert_slice, axis=1)
    gate_part = jnp.sum(cotangent.astype(jnp.float32)[:, None, :] * expert_slice, axis=2)
    gate_grad = lax.psum_scatter(gate_part, "dp", scatter_dimension=1, tiled=True)
    return (
        layer_out.astype(jnp.bfloat16),
        token_grad.astype(jnp.bfloat16),
        gate_grad,
        w_gate_grad,
        w_up_grad,
        w_down_grad,
    )


def solution(mesh):
    in_specs = (
        P("expert", "dp"),
        P("expert", "dp"),
        P("expert", None),
        P("expert", None),
        P(),
        P("expert", "dp", None),
        P("expert", "dp", None),
        P("expert", "dp", None),
    )
    out_specs = (
        P("expert", "dp"),
        P("expert", "dp"),
        P("expert", "dp"),
        P("expert", "dp", None),
        P("expert", "dp", None),
        P("expert", "dp", None),
    )
    return jax.shard_map(body, mesh=mesh, in_specs=in_specs, out_specs=out_specs, check_vma=False)
```

profile of v0, /device:TPU:0, one launch (start us, length us, event | category | flops | bytes accessed | tf_op | source)
XLA Modules:
  0.0 345.2 jit_solution(2087983835047656661)
XLA Ops:
  9.1 6.8 %reduce-window.6 = s32[24,8,128]{2,1,0:T(8,128)S(1)} reduce-window(s32[24,8,128]{2,1,0:T(8,128)S(1)} %fusion.18, s32[]{:T(128)} %constant.53.clone.1), window={size=1x1x128 pad=0_0x0_0x127_0}, to_apply=%region_0.0 | reduce-window | flops 3121152 | bytes 196612 | tf_op jit(solution)/shard_map/reduce-window
  16.4 4.3 %scatter_custom_fusion = s32[1056]{0:T(1024)S(1)} fusion(s32[1024]{0:T(1024)S(1)} %bitcast.86, s32[1024]{0:T(1024)S(1)} %iota.16, s32[]{:T(128)} %constant.51.clone.1), kind=kCustom, calls=%fused_computation.71 | custom fusion | bytes 4228 | tf_op jit(solution)/shard_map/scatter | solution.py:52
  21.6 4.2 %gather_fusion = bf16[1056,512]{1,0:T(8,128)(2,1)S(1)} fusion(bf16[129,512]{1,0:T(8,128)(2,1)S(1)} %concatenate.50, s32[2048]{0:T(1024)S(1)} %get-tuple-element.27), kind=kCustom, calls=%fused_computation | custom fusion | bytes 2166912 | tf_op jit(solution)/shard_map/gather | solution.py:61
  26.3 36.0 %all_to_all.54 = bf16[8,3,44,512]{3,2,1,0:T(8,128)(2,1)S(1)} all-to-all(bf16[8,3,44,512]{3,2,1,0:T(8,128)(2,1)S(1)} %maximum_maximum_fusion.2), channel_id=1, replica_groups=mesh['dp'=4,'expert'=8] {'expert'}, dimensions={0} | all-to-all | bytes 2162688 | tf_op jit(solution)/shard_map/all_to_all | solution.py:66
  64.4 6.2 %gather_fusion.2 = f32[1056]{0:T(1024)S(1)} fusion(f32[1025]{0:T(1024)S(1)} %pad_maximum_fusion.11, s32[2048]{0:T(1024)S(1)} %get-tuple-element.26), kind=kCustom, calls=%fused_computation.2 | custom fusion | bytes 12672 | tf_op jit(solution)/shard_map/gather | solution.py:55
  70.7 4.2 %gather_fusion.3 = bf16[1056,512]{1,0:T(8,128)(2,1)S(1)} fusion(bf16[129,512]{1,0:T(8,128)(2,1)S(1)} %concatenate.60, s32[2048]{0:T(1024)S(1)} %get-tuple-element.27), kind=kCustom, calls=%fused_computation.3 | custom fusion | bytes 2166912 | tf_op jit(solution)/shard_map/gather | solution.py:62
  75.6 31.8 %all_to_all.55 = bf16[8,3,44,512]{3,2,1,0:T(8,128)(2,1)S(1)} all-to-all(bf16[8,3,44,512]{3,2,1,0:T(8,128)(2,1)S(1)} %maximum_maximum_fusion.3), channel_id=1, replica_groups=mesh['dp'=4,'expert'=8] {'expert'}, dimensions={0} | all-to-all | bytes 2162688 | tf_op jit(solution)/shard_map/all_to_all | solution.py:67
  111.5 2.7 constant_dynamic-slice_fusion
  116.3 9.8 %fusion.9 = f32[3,352,768]{2,1,0:T(8,128)} fusion(bf16[1,3,352,2048]{3,2,1,0:T(8,128)(2,1)} %all-gather.3.cloned.1.call-done, bf16[1,768,2048]{2,1,0:T(8,128)(2,1)S(1)} %maximum_bitcast_fusion, bf16[2,384,2048]{2,1,0:T(8,128)(2,1)} %param.14, bf16[2,384,2048]{2,1,0:T(8,128)(2,1)} %param.13), kind=kOutput, calls=%fused_computation.20 | convolution fusion | flops 3350200320 | bytes 17006592 | tf_op jit(solution)/shard_map/cmd,cfd->cmf/dot_general | solution.py:9
  126.1 16.5 %all-gather.5.cloned.1.call-done = bf16[1,3,352,2048]{3,2,1,0:T(8,128)(2,1)} async-done(((bf16[1,3,352,512]{3,2,1,0:T(8,128)(2,1)}), bf16[1,3,352,2048]{3,2,1,0:T(8,128)(2,1)}) %all-gather.5.cloned.1.call-update) | async-done | bytes 4325392 | tf_op jit(solution)/shard_map/all_gather | solution.py:71
  142.6 8.3 %multiply_convert_fusion.2 = (bf16[3,352,384]{2,1,0:T(8,128)(2,1)S(1)}, bf16[3,352,384]{2,1,0:T(8,128)(2,1)S(1)}, bf16[3,352,384]{2,1,0:T(8,128)(2,1)}) fusion(f32[3,352,768]{2,1,0:T(8,128)} %fusion.9, bf16[1,384,2048]{2,1,0:T(8,128)(2,1)} %constant_dynamic-slice_fusion, bf16[2,384,2048]{2,1,0:T(8,128)(2,1)} %param.15, ...), kind=kOutput, calls=%fused_computation.41 | convolution fusion | flops 1669386240 | bytes 14721024 | tf_op jit(solution)/shard_map/cmd,cfd->cmf/dot_general | solution.py:16
  152.1 7.6 %fusion.12 = bf16[3,352,2048]{2,1,0:T(8,128)(2,1)} fusion(bf16[1,768,2048]{2,1,0:T(8,128)(2,1)S(1)} %maximum_bitcast_fusion, bf16[2,384,2048]{2,1,0:T(8,128)(2,1)S(1)} %copy-done.12, bf16[2,384,2048]{2,1,0:T(8,128)(2,1)S(1)} %copy-done.13, bf16[3,352,384]{2,1,0:T(8,128)(2,1)S(1)} %get-tuple-element.13, bf16[3,352,384]{2,1,0:T(8,128)(2,1)S(1)} %get-tuple-element.12), kind=kOutput, calls=%fused_computation.23 | convolution fusion | flops 3355607040 | bytes 15384576 | tf_op jit(solution)/shard_map/cmf,cfd->cmd/dot_general | solution.py:22
  161.3 6.3 %convolution_convert_fusion = bf16[3,352,2048]{2,1,0:T(8,128)(2,1)} fusion(bf16[3,352,384]{2,1,0:T(8,128)(2,1)S(1)} %copy-done.10, bf16[1,384,2048]{2,1,0:T(8,128)(2,1)S(1)} %copy-done.4, bf16[2,384,2048]{2,1,0:T(8,128)(2,1)} %param.15), kind=kOutput, calls=%fused_computation.24 | convolution fusion | flops 1665466368 | bytes 9854976 | tf_op jit(solution)/shard_map/cmf,cfd->cmd/dot_general | solution.py:15
  170.6 8.8 %fusion.3 = f32[3,384,2048]{2,1,0:T(8,128)} fusion(bf16[3,352,384]{2,1,0:T(8,128)(2,1)S(1)} %copy-done.10, bf16[1,3,352,2048]{3,2,1,0:T(8,128)(2,1)} %all-gather.5.cloned.1.call-done), kind=kOutput, calls=%fused_computation.14 | convolution fusion | flops 1660944384 | bytes 14573568 | tf_op jit(solution)/shard_map/cmf,cmd->cfd/dot_general | solution.py:24
  179.4 25.7 %reduce-scatter.5.cloned.1.call-done = bf16[3,352,512]{2,1,0:T(8,128)(2,1)} async-done(((bf16[3,352,2048]{2,1,0:T(8,128)(2,1)}), bf16[3,352,512]{2,1,0:T(8,128)(2,1)}) %reduce-scatter.5.cloned.1.call-update) | async-done | bytes 1081360 | tf_op jit(solution)/shard_map/reduce_scatter | solution.py:98
  205.2 3.4 copy.76
  208.6 5.5 %all-to-all-start.3 = ((bf16[1,3,352,512]{3,1,0,2:T(4,128)(2,1)}), bf16[1,3,352,512]{3,1,0,2:T(4,128)(2,1)}, u32[]{:S(2)}, u32[]{:S(2)}) async-start(bf16[1,3,352,512]{3,1,0,2:T(4,128)(2,1)} %copy.76), calls=%async_computation.5 | async-start | bytes 2883584 | tf_op jit(solution)/shard_map/all_to_all | solution.py:106
  214.1 7.2 %fusion.7 = f32[3,768,2048]{2,1,0:T(8,128)S(1)} fusion(bf16[1,3,352,2048]{3,2,1,0:T(8,128)(2,1)} %all-gather.3.cloned.1.call-done, bf16[3,352,384]{2,1,0:T(8,128)(2,1)S(1)} %copy-done.9, bf16[3,352,384]{2,1,0:T(8,128)(2,1)S(1)} %copy-done.7), kind=kOutput, calls=%fused_computation.18 | convolution fusion | flops 3325132800 | bytes 24821760 | tf_op jit(solution)/shard_map/cmf,cmd->cfd/dot_general | solution.py:23
  221.3 6.9 %copy-done = f32[3,768,2048]{2,1,0:T(8,128)} copy-done((f32[3,768,2048]{2,1,0:T(8,128)}, f32[3,768,2048]{2,1,0:T(8,128)S(1)}, u32[]{:S(2)}) %copy-start) | copy-done | bytes 18874392
  230.5 22.6 %reduce-scatter.3.cloned.1.call-done = bf16[3,352,512]{2,1,0:T(8,128)(2,1)} async-done(((bf16[3,352,2048]{2,1,0:T(8,128)(2,1)}), bf16[3,352,512]{2,1,0:T(8,128)(2,1)}) %reduce-scatter.3.cloned.1.call-update) | async-done | bytes 1081360 | tf_op jit(solution)/shard_map/reduce_scatter | solution.py:95
  253.1 3.3 copy.70
  256.5 5.8 %all-to-all-start.1 = ((bf16[1,3,352,512]{3,1,0,2:T(4,128)(2,1)}), bf16[1,3,352,512]{3,1,0,2:T(4,128)(2,1)}, u32[]{:S(2)}, u32[]{:S(2)}) async-start(bf16[1,3,352,512]{3,1,0,2:T(4,128)(2,1)} %copy.70), calls=%async_computation.2 | async-start | bytes 2883584 | tf_op jit(solution)/shard_map/all_to_all | solution.py:103
  265.1 10.6 %fusion.1 = (bf16[2,384,2048]{2,1,0:T(8,128)(2,1)}, bf16[2,384,2048]{2,1,0:T(8,128)(2,1)}, bf16[2,384,2048]{2,1,0:T(8,128)(2,1)}) fusion(f32[3,768,2048]{2,1,0:T(8,128)} %copy-done, f32[384,2048]{1,0:T(8,128)S(1)} %get-tuple-element.10, f32[2]{0:T(128)S(1)} %compare_convert_fusion, f32[384,2048]{1,0:T(8,128)S(1)} %copy-done.1, ...), kind=kLoop, calls=%fused_computation.10 | loop fusion | flops 14155776 | bytes 37748744 | tf_op jit(solution)/shard_map/convert_element_type | solution.py:92
  277.4 3.6 %reshape.130 = f32[1,3,8,44,512]{4,0,3,2,1:T(1,128)} reshape(f32[1,3,352,512]{3,2,1,0:T(8,128)S(1)} %copy_convert_fusion) | data formatting | bytes 4325376 | tf_op jit(solution)/shard_map/convert_element_type | solution.py:112
  284.7 11.9 %all-to-all-done.1 = bf16[1,3,352,512]{3,1,0,2:T(4,128)(2,1)} async-done(((bf16[1,3,352,512]{3,1,0,2:T(4,128)(2,1)}), bf16[1,3,352,512]{3,1,0,2:T(4,128)(2,1)}, u32[]{:S(2)}, u32[]{:S(2)}) %all-to-all-start.1) | async-done | bytes 1081376 | tf_op jit(solution)/shard_map/all_to_all | solution.py:103
  298.3 3.6 %reshape.129 = f32[1,3,8,44,512]{4,0,3,2,1:T(1,128)} reshape(f32[1,3,352,512]{3,2,1,0:T(8,128)S(1)} %copy_convert_fusion.1) | data formatting | bytes 4325376 | tf_op jit(solution)/shard_map/convert_element_type | solution.py:105
  306.6 2.7 copy.79
  311.0 4.9 %gather_fusion.4 = f32[1024,512]{1,0:T(8,128)} fusion(f32[1056,512]{1,0:T(8,128)S(1)} %reshape.124, s32[1024]{0:T(1024)S(1)} %broadcast_clamp_fusion), kind=kCustom, calls=%fused_computation.4 | custom fusion | bytes 4198400 | tf_op jit(solution)/shard_map/gather | solution.py:119
  315.9 2.9 bitcast_reduce_fusion
  323.6 4.9 %gather_fusion.1 = f32[1024,512]{1,0:T(8,128)} fusion(f32[1056,512]{1,0:T(8,128)S(1)} %reshape.121, s32[1024]{0:T(1024)S(1)} %broadcast_clamp_fusion), kind=kCustom, calls=%fused_computation.1 | custom fusion | bytes 4198400 | tf_op jit(solution)/shard_map/gather | solution.py:116
  328.5 3.1 fusion.14
  331.7 5.9 %all-reduce.2 = f32[128,8]{0,1:T(8,128)S(1)} all-reduce(f32[128,8]{0,1:T(8,128)S(1)} %copy.80), channel_id=4, replica_groups=mesh['dp'=4,'expert'=8] {'dp'}, use_global_device_ids=true, to_apply=%region_9.10.clone | all-reduce | flops 1024 | bytes 8192
  (112 shorter events, 39.7 us)
Async XLA Ops:
  7.2 109.2 %all-gather.3.cloned.1.call-start = ((), (), s32[]{:S(2)}) async-start(), calls=%async_computation.6 | async-start | bytes 5406720 | tf_op jit(solution)/shard_map/all_gather | solution.py:70
  62.3 1.3 copy-start.18
  63.5 79.1 %all-gather.5.cloned.1.call-start = ((), (), s32[]{:S(2)}) async-start(), calls=%async_computation.8 | async-start | bytes 5406720 | tf_op jit(solution)/shard_map/all_gather | solution.py:71
  63.7 0.6 copy-start.14
  64.4 6.3 %copy-start.16 = (bf16[128,512]{1,0:T(8,128)(2,1)S(1)}, bf16[128,512]{1,0:T(8,128)(2,1)}, u32[]{:S(2)}) copy-start(bf16[128,512]{1,0:T(8,128)(2,1)} %param.9) | copy-start | bytes 393220
  107.4 1.4 copy-start.19
  108.6 5.6 %copy-start.11 = (bf16[2,384,2048]{2,1,0:T(8,128)(2,1)S(1)}, bf16[2,384,2048]{2,1,0:T(8,128)(2,1)}, u32[]{:S(2)}) copy-start(bf16[2,384,2048]{2,1,0:T(8,128)(2,1)} %param.14) | copy-start | bytes 9437188
  108.6 96.6 %reduce-scatter.5.cloned.1.call-start = ((), (), s32[]{:S(2)}) async-start(), calls=%async_computation.9 | async-start | bytes 5406720 | tf_op jit(solution)/shard_map/reduce_scatter | solution.py:98
  142.6 9.5 %copy-start.12 = (bf16[2,384,2048]{2,1,0:T(8,128)(2,1)S(1)}, bf16[2,384,2048]{2,1,0:T(8,128)(2,1)}, u32[]{:S(2)}) copy-start(bf16[2,384,2048]{2,1,0:T(8,128)(2,1)} %param.14) | copy-start | bytes 9437188
  142.6 9.5 %copy-start.13 = (bf16[2,384,2048]{2,1,0:T(8,128)(2,1)S(1)}, bf16[2,384,2048]{2,1,0:T(8,128)(2,1)}, u32[]{:S(2)}) copy-start(bf16[2,384,2048]{2,1,0:T(8,128)(2,1)} %param.13) | copy-start | bytes 9437188
  150.9 0.9 copy-start.6
  150.9 1.2 copy-start.8
  159.7 1.4 copy-start.4
  159.7 1.6 copy-start.10
  159.7 93.4 %reduce-scatter.3.cloned.1.call-start = ((), (), s32[]{:S(2)}) async-start(), calls=%async_computation.7 | async-start | bytes 5406720 | tf_op jit(solution)/shard_map/reduce_scatter | solution.py:95
  167.7 1.0 copy-start.17
  167.7 1.0 copy-start.20
  205.2 8.9 %copy-start.7 = (bf16[3,352,384]{2,1,0:T(8,128)(2,1)S(1)}, bf16[3,352,384]{2,1,0:T(8,128)(2,1)}, u32[]{:S(2)}) copy-start(bf16[3,352,384]{2,1,0:T(8,128)(2,1)} %copy-done.6) | copy-start | bytes 2433028
  205.2 8.9 %copy-start.9 = (bf16[3,352,384]{2,1,0:T(8,128)(2,1)S(1)}, bf16[3,352,384]{2,1,0:T(8,128)(2,1)}, u32[]{:S(2)}) copy-start(bf16[3,352,384]{2,1,0:T(8,128)(2,1)} %copy-done.8) | copy-start | bytes 2433028
  208.6 47.9 %all-to-all-start.3 = ((bf16[1,3,352,512]{3,1,0,2:T(4,128)(2,1)}), bf16[1,3,352,512]{3,1,0,2:T(4,128)(2,1)}, u32[]{:S(2)}, u32[]{:S(2)}) async-start(bf16[1,3,352,512]{3,1,0,2:T(4,128)(2,1)} %copy.76), calls=%async_computation.5 | async-start | bytes 2883584 | tf_op jit(solution)/shard_map/all_to_all | solution.py:106
  221.3 7.0 %copy-start = (f32[3,768,2048]{2,1,0:T(8,128)}, f32[3,768,2048]{2,1,0:T(8,128)S(1)}, u32[]{:S(2)}) copy-start(f32[3,768,2048]{2,1,0:T(8,128)S(1)} %fusion.7) | copy-start | bytes 56623108
  256.5 40.1 %all-to-all-start.1 = ((bf16[1,3,352,512]{3,1,0,2:T(4,128)(2,1)}), bf16[1,3,352,512]{3,1,0,2:T(4,128)(2,1)}, u32[]{:S(2)}, u32[]{:S(2)}) async-start(bf16[1,3,352,512]{3,1,0,2:T(4,128)(2,1)} %copy.70), calls=%async_computation.2 | async-start | bytes 2883584 | tf_op jit(solution)/shard_map/all_to_all | solution.py:103
  262.3 2.8 copy-start.1
  304.2 2.1 copy-start.2
  315.9 2.9 copy-start.3
  315.9 2.9 copy-start.5
  323.6 4.9 %copy-start.15 = (f32[128,8]{1,0:T(8,128)S(1)}, f32[128,8]{1,0:T(8,128)}, u32[]{:S(2)}) copy-start(f32[128,8]{1,0:T(8,128)} %copy-done.14) | copy-start | bytes 12292
Sparse Core Ops, SparseCore 0:
  63.6 33.8 all-gather.2
  108.7 33.8 all-gather.4
  159.8 45.2 reduce-scatter.4
  207.8 45.3 reduce-scatter.2
where the time goes:
time: 350 us; the launch traced here: 345 us
  local copies, waits for them, and re-layouts  87.6 us (25%)
  waiting for transfers between devices  76.8 us (22%)
  blocking collectives  73.8 us (21%)
  matrix products  48 us (14%)
  other arithmetic  29.7 us (8%)
  between operations  17.4 us (5%)
  starting transfers between devices  11.9 us (3%)
    all_to_all x1, blocking collectives, body(): lax.all_to_all(send_in, 'expert', split_axis=0, concat_axis=2, tiled=True)  36 us
    all_to_all x1, blocking collectives, body(): lax.all_to_all(send_cot, 'expert', split_axis=0, concat_axis=2, tiled=True)  31.8 us
    reduce_scatter x1, waiting for transfers between devices, body(): lax.psum_scatter(back_rows.astype(jnp.bfloat16), 'dp', scatter_dimension=...  25.7 us
    reduce_scatter x1, waiting for transfers between devices, body(): lax.psum_scatter(out_rows.astype(jnp.bfloat16), 'dp', scatter_dimension=2...  22.6 us
    all_gather x1, waiting for transfers between devices, body(): lax.all_gather(thin_cot, 'dp', axis=3, tiled=True)  16.5 us
    unnamed x46, local copies, waits for them, and re-layouts  13.7 us
    all_to_all x1, waiting for transfers between devices, body(): lax.all_to_all(summed_out[None].astype(jnp.bfloat16), 'expert', split_axi...  11.9 us
    convert_element_type x4, local copies, waits for them, and re-layouts, body(): got_out, got_back = (lax.all_to_all(summed_out[None].astype(jnp.bfloat16)...  11.8 us
  transfers between devices with their start and end apart: 6, of which 4 were waited for; matrix products, arithmetic and copies ran while one was open for 23% of the time, Pallas kernels for 0%

commit v1 on v0

v1 whole, which is shorter than its diff:
```python
import jax
import jax.numpy as jnp
from jax import lax
from jax.sharding import PartitionSpec as P


def body(tokens, cotangent, route, gate_prob, replica_pick, w_gate, w_up, w_down):
    groups = lax.axis_size("expert")
    column = lax.axis_index("expert")
    tok_dev, slice_width = tokens.shape
    fanout = route.shape[1]
    owned, width, features = w_gate.shape
    local_copies = owned + 1
    copies = groups * local_copies
    capacity = tok_dev * fanout // copies + 2
    half_axis = groups // 2
    rows = groups * capacity
    total = groups * tok_dev
    f32, bf16 = jnp.float32, jnp.bfloat16

    all_route = lax.all_gather(route, "expert", axis=0, tiled=True)
    all_gate = lax.all_gather(gate_prob, "expert", axis=0, tiled=True)
    tok = lax.all_gather(tokens, "expert", axis=0, tiled=True)
    tok = lax.all_gather(tok, "dp", axis=1, tiled=True)
    cot = lax.all_gather(cotangent, "expert", axis=0, tiled=True)
    cot = lax.all_gather(cot, "dp", axis=1, tiled=True)

    partner = (column + half_axis) % groups
    own_pick = replica_pick[partner]
    select = [(own_pick == j).astype(bf16) for j in range(owned)]
    copy_ids = [column * local_copies + j for j in range(owned)] + [partner * local_copies + owned]

    route_t = all_route.T
    gate_t = all_gate.T
    hits = [route_t == c for c in copy_ids]
    member = jnp.stack([jnp.sum(h.astype(f32), axis=0) for h in hits])
    gate_of = jnp.stack([jnp.sum(jnp.where(h, gate_t, 0.0), axis=0) for h in hits])
    blocks = member.reshape(local_copies, groups, tok_dev)
    tri = (jnp.arange(tok_dev)[:, None] <= jnp.arange(tok_dev)[None, :]).astype(bf16)
    inside = jnp.einsum("cgt,tu->cgu", blocks.astype(bf16), tri, preferred_element_type=f32)
    sums = jnp.sum(blocks, axis=2)
    before = (jnp.arange(groups)[:, None] < jnp.arange(groups)[None, :]).astype(f32)
    offset = jnp.sum(sums[:, :, None] * before[None], axis=1)
    place = (inside + offset[:, :, None]).reshape(local_copies, total) - 1.0
    place = jnp.where(member > 0, place, -1.0).astype(jnp.int32)
    picks = place[:, None, :] == jnp.arange(rows, dtype=jnp.int32)[None, :, None]
    pick = picks.astype(bf16)
    gate_rows = jnp.sum(jnp.where(picks, gate_of[:, None, :], 0.0), axis=2)

    chosen = [lax.dynamic_index_in_dim(w, own_pick, 0, keepdims=True) for w in (w_gate, w_up, w_down)]
    gate_w = jnp.concatenate([w_gate, chosen[0]], axis=0)
    up_w = jnp.concatenate([w_up, chosen[1]], axis=0)
    down_w = jnp.concatenate([w_down, chosen[2]], axis=0)

    rows_in = jnp.einsum("crt,td->crd", pick, tok, preferred_element_type=f32).astype(bf16)
    gate_act = jnp.einsum("crd,cfd->crf", rows_in, gate_w, preferred_element_type=f32)
    up_act = jnp.einsum("crd,cfd->crf", rows_in, up_w, preferred_element_type=f32)
    sig = jax.nn.sigmoid(gate_act)
    activated = gate_act * sig
    hidden = activated * up_act
    g = gate_rows[:, :, None]
    hidden_g = (g * hidden).astype(bf16)
    out_rows = jnp.einsum("crf,cfd->crd", hidden_g, down_w, preferred_element_type=f32).astype(bf16)
    out_tok = jnp.einsum("crt,crd->td", pick, out_rows, preferred_element_type=f32).astype(bf16)
    out_dp = lax.psum_scatter(out_tok, "dp", scatter_dimension=1, tiled=True)
    layer_out = lax.psum_scatter(out_dp, "expert", scatter_dimension=0, tiled=True)

    rows_cot = jnp.einsum("crt,td->crd", pick, cot, preferred_element_type=f32).astype(bf16)
    back_h = jnp.einsum("crd,cfd->crf", rows_cot, down_w, preferred_element_type=f32)
    gg_rows = jnp.sum(hidden * back_h, axis=2)
    d_hidden = g * back_h
    d_gate = (d_hidden * up_act * sig * (1.0 + gate_act * (1.0 - sig))).astype(bf16)
    d_up = (d_hidden * activated).astype(bf16)
    back_rows = jnp.einsum("crf,cfd->crd", d_gate, gate_w, preferred_element_type=f32)
    back_rows = back_rows + jnp.einsum("crf,cfd->crd", d_up, up_w, preferred_element_type=f32)
    back_tok = jnp.einsum("crt,crd->td", pick, back_rows.astype(bf16), preferred_element_type=f32).astype(bf16)
    back_dp = lax.psum_scatter(back_tok, "dp", scatter_dimension=1, tiled=True)
    token_grad = lax.psum_scatter(back_dp, "expert", scatter_dimension=0, tiled=True)

    gg_tok = jnp.sum(jnp.where(picks, gg_rows[:, :, None], 0.0), axis=1)
    gg = sum(jnp.where(h, gg_tok[j][None], 0.0) for j, h in enumerate(hits))
    gg = lax.psum_scatter(gg, "expert", scatter_dimension=1, tiled=True)
    gate_grad = lax.psum_scatter(gg, "dp", scatter_dimension=0, tiled=True).T

    def weight_grad(left, right):
        parts = []
        for j in range(owned):
            both_l = jnp.concatenate([left[j], left[owned] * select[j]], axis=0)
            both_r = jnp.concatenate([right[j], right[owned]], axis=0)
            parts.append(jnp.einsum("rf,rd->fd", both_l, both_r, preferred_element_type=f32).astype(bf16))
        return jnp.stack(parts)

    return (
        layer_out,
        token_grad,
        gate_grad,
        weight_grad(d_gate, rows_in),
        weight_grad(d_up, rows_in),
        weight_grad(hidden_g, rows_cot),
    )


def solution(mesh):
    in_specs = (
        P("expert", "dp"),
        P("expert", "dp"),
        P("expert", None),
        P("expert", None),
        P(),
        P("expert", "dp", None),
        P("expert", "dp", None),
        P("expert", "dp", None),
    )
    out_specs = (
        P("expert", "dp"),
        P("expert", "dp"),
        P("expert", "dp"),
        P("expert", "dp", None),
        P("expert", "dp", None),
        P("expert", "dp", None),
    )
    return jax.shard_map(body, mesh=mesh, in_specs=in_specs, out_specs=out_specs, check_vma=False)
```

time: 350 us -> 494 us (1.41)
  waiting for transfers between devices: 76.8 us -> 312 us
  local copies, waits for them, and re-layouts: 87.6 us -> 16 us
  matrix products: 48 us -> 68.6 us
  other arithmetic: 29.7 us -> 11.6 us
  starting transfers between devices: 11.9 us -> 0.35 us
  blocking collectives: 73.8 us -> 66.8 us
    reduce_scatter x2 -> x5, waiting for transfers between devices: 48.4 us -> 225 us  [the longest x1 66.7 us: body(): lax.psum_scatter(back_dp, 'expert', scatter_dimension=0, tiled=True)]
    all_gather x2 -> x4, waiting for transfers between devices: 16.5 us -> 85.3 us  [the longest x1 44.3 us: body(): tok = lax.all_gather(tokens, 'expert', axis=0, tiled=True)]
    all_to_all x2 -> x0, blocking collectives: 67.8 us -> none  [the longest x1 36 us: body(): lax.all_to_all(send_in, 'expert', split_axis=0, concat_axis=2, tiled=True)]
    all_gather x0 -> x2, blocking collectives: none -> 61.1 us  [the longest x1 30.5 us: body(): all_route = lax.all_gather(route, 'expert', axis=0, tiled=True)]
    gather x5 -> x0, local copies, waits for them, and re-layouts: 24.3 us -> none  [the longest x1 6.17 us: body(): jnp.concatenate([gate_prob.reshape(-1), jnp.zeros((1,), jnp.float32)], ax...]
    dot_general x6 -> x15, matrix products: 48 us -> 68.6 us  [the longest x6 12.9 us: weight_grad(): jnp.einsum('rf,rd->fd', both_l, both_r, preferred_element_type=f32)]
    convert_element_type x7 -> x0, local copies, waits for them, and re-layouts: 18.7 us -> none  [the longest x4 11.8 us: body(): got_out, got_back = (lax.all_to_all(summed_out[None].astype(jnp.bfloat16)...]
    convert_element_type x7 -> x3, other arithmetic: 14.9 us -> 2.47 us  [the longest x1 2.4 us: body(): d_up = (d_hidden * activated).astype(bf16)]
  transfers between devices with their start and end apart: 6 -> 9, of which waited for: 4 -> 7; matrix products, arithmetic and copies ran while one was open for 23% -> 14% of each run, Pallas kernels for 0% -> 0%
where the time goes in v1:
time: 494 us; the launch traced here: 493 us
  waiting for transfers between devices  312 us (63%)
  matrix products  68.6 us (14%)
  blocking collectives  66.8 us (14%)
  between operations  18.1 us (4%)
  local copies, waits for them, and re-layouts  16 us (3%)
  other arithmetic  11.6 us (2%)
    reduce_scatter x1, waiting for transfers between devices, body(): lax.psum_scatter(back_dp, 'expert', scatter_dimension=0, tiled=True)  66.7 us
    reduce_scatter x1, waiting for transfers between devices, body(): lax.psum_scatter(out_dp, 'expert', scatter_dimension=0, tiled=True)  60.1 us
    all_gather x1, waiting for transfers between devices, body(): tok = lax.all_gather(tokens, 'expert', axis=0, tiled=True)  44.3 us
    reduce_scatter x1, waiting for transfers between devices, body(): gg = lax.psum_scatter(gg, 'expert', scatter_dimension=1, tiled=True)  43.8 us
    all_gather x1, waiting for transfers between devices, body(): cot = lax.all_gather(cotangent, 'expert', axis=0, tiled=True)  41 us
    reduce_scatter x1, waiting for transfers between devices, body(): back_dp = lax.psum_scatter(back_tok, 'dp', scatter_dimension=1, tiled=True)  33.9 us
    all_gather x1, blocking collectives, body(): all_route = lax.all_gather(route, 'expert', axis=0, tiled=True)  30.5 us
    all_gather x1, blocking collectives, body(): all_gate = lax.all_gather(gate_prob, 'expert', axis=0, tiled=True)  30.5 us
  transfers between devices with their start and end apart: 9, of which 7 were waited for; matrix products, arithmetic and copies ran while one was open for 14% of the time, Pallas kernels for 0%

profile of v1, /device:TPU:0, one launch (start us, length us, event | category | flops | bytes accessed | tf_op | source)
XLA Modules:
  0.0 493.1 jit_solution(10632463650866880326)
XLA Ops:
  8.7 44.3 %all-gather.5.cloned.1.call-done = bf16[1024,512]{1,0:T(8,128)(2,1)} async-done(((bf16[128,512]{1,0:T(8,128)(2,1)}), bf16[1024,512]{1,0:T(8,128)(2,1)}) %all-gather.5.cloned.1.call-update) | async-done | bytes 1048592 | tf_op jit(solution)/shard_map/all_gather | solution.py:23
  53.1 41.0 %all-gather.9.cloned.1.call-done = bf16[1024,512]{1,0:T(8,128)(2,1)} async-done(((bf16[128,512]{1,0:T(8,128)(2,1)}), bf16[1024,512]{1,0:T(8,128)(2,1)}) %all-gather.9.cloned.1.call-update) | async-done | bytes 1048592 | tf_op jit(solution)/shard_map/all_gather | solution.py:25
  97.4 30.5 %all_gather.18 = s32[1024,8]{0,1:T(8,128)S(1)} all-gather(s32[128,8]{0,1:T(8,128)} %param.10), channel_id=1, replica_groups=mesh['dp'=4,'expert'=8] {'expert'}, dimensions={0}, use_global_device_ids=true | all-gather | bytes 36864 | tf_op jit(solution)/shard_map/all_gather | solution.py:21
  127.9 30.5 %all_gather.19 = f32[1024,8]{0,1:T(8,128)S(1)} all-gather(f32[128,8]{0,1:T(8,128)} %param.11), channel_id=1, replica_groups=mesh['dp'=4,'expert'=8] {'expert'}, dimensions={0}, use_global_device_ids=true | all-gather | bytes 36864 | tf_op jit(solution)/shard_map/all_gather | solution.py:22
  158.9 2.9 constant_dynamic-slice_fusion
  161.8 2.7 constant_dynamic-slice_fusion.1
  165.8 7.1 %fusion.7 = bf16[3,352,2048]{2,1,0:T(8,128)(2,1)S(1)} fusion(bf16[1024,2048]{1,0:T(8,128)(2,1)} %all-gather.7.cloned.1.call-done, s32[3,1024]{1,0:T(4,128)S(1)} %fusion.59), kind=kOutput, calls=%fused_computation.16 | convolution fusion | flops 4432429056 | bytes 8531968 | tf_op jit(solution)/shard_map/crt,td->crd/dot_general | solution.py:55
  173.0 3.6 fusion.19
  177.5 2.4 fusion.17
  180.0 7.8 %fusion.10 = bf16[3,352,2048]{2,1,0:T(8,128)(2,1)S(1)} fusion(bf16[1024,2048]{1,0:T(8,128)(2,1)} %all-gather.11.cloned.1.call-done, s32[3,1024]{1,0:T(4,128)S(1)} %fusion.59), kind=kOutput, calls=%fused_computation.17 | convolution fusion | flops 4432429056 | bytes 8531968 | tf_op jit(solution)/shard_map/crt,td->crd/dot_general | solution.py:68
  187.9 2.6 multiply_reduce_fusion
  190.4 1.4 select_reduce_fusion
  191.8 2.4 multiply_convert_fusion
  195.1 11.1 %bitcast_convert_fusion.1 = bf16[1024,2048]{1,0:T(8,128)(2,1)} fusion(s32[3,1024]{1,0:T(4,128)S(1)} %fusion.59, bf16[3,352,384]{2,1,0:T(8,128)(2,1)S(1)} %get-tuple-element.25, bf16[1,384,2048]{2,1,0:T(8,128)(2,1)} %constant_dynamic-slice_fusion, bf16[2,384,2048]{2,1,0:T(8,128)(2,1)} %param.15), kind=kOutput, calls=%fused_computation.2 | convolution fusion | flops 6097829888 | bytes 9736192 | tf_op jit(solution)/shard_map/crt,crd->td/dot_general | solution.py:64
  207.6 8.5 %fusion.18 = f32[3,352,2048]{2,1,0:T(8,128)} fusion(bf16[3,352,384]{2,1,0:T(8,128)(2,1)S(1)} %get-tuple-element.24, bf16[1,384,2048]{2,1,0:T(8,128)(2,1)S(1)} %copy-done.2, bf16[2,384,2048]{2,1,0:T(8,128)(2,1)} %param.13), kind=kOutput, calls=%fused_computation.28 | convolution fusion | flops 1663303680 | bytes 14180352 | tf_op jit(solution)/shard_map/crf,cfd->crd/dot_general | solution.py:74
  216.1 12.5 %bitcast_convert_fusion = bf16[1024,2048]{1,0:T(8,128)(2,1)} fusion(f32[3,352,2048]{2,1,0:T(8,128)} %fusion.18, bf16[3,352,384]{2,1,0:T(8,128)(2,1)S(1)} %get-tuple-element.23, bf16[1,384,2048]{2,1,0:T(8,128)(2,1)} %constant_dynamic-slice_fusion.1, bf16[2,384,2048]{2,1,0:T(8,128)(2,1)} %param.14, s32[3,1024]{1,0:T(4,128)S(1)} %fusion.59), kind=kOutput, calls=%fused_computation.1 | convolution fusion | flops 6099992576 | bytes 18386944 | tf_op jit(solution)/shard_map/crt,crd->td/dot_general | solution.py:76
  229.5 20.2 %reduce-scatter.6.cloned.1.call-done = bf16[1024,512]{1,0:T(8,128)(2,1)} async-done(((bf16[1024,2048]{1,0:T(8,128)(2,1)}), bf16[1024,512]{1,0:T(8,128)(2,1)}) %reduce-scatter.6.cloned.1.call-update) | async-done | bytes 1048592 | tf_op jit(solution)/shard_map/reduce_scatter | solution.py:65
  252.3 2.6 slice_bitcast_fusion.5
  254.9 1.4 fusion.26
  257.7 2.6 fusion.28
  260.3 2.6 fusion.27
  262.9 33.9 %reduce-scatter.10.cloned.1.call-done = bf16[1024,512]{1,0:T(8,128)(2,1)} async-done(((bf16[1024,2048]{1,0:T(8,128)(2,1)}), bf16[1024,512]{1,0:T(8,128)(2,1)}) %reduce-scatter.10.cloned.1.call-update) | async-done | bytes 1048592 | tf_op jit(solution)/shard_map/reduce_scatter | solution.py:77
  296.8 3.4 fusion.29
  300.8 1.5 fusion.30
  302.3 1.4 fusion.31
  303.7 1.9 pad_maximum_fusion.7
  305.7 1.9 pad_maximum_fusion.9
  307.6 1.9 pad_maximum_fusion.8
  309.6 43.8 %reduce-scatter.14.cloned.1.call-done = f32[8,128]{1,0:T(8,128)} async-done(((f32[8,1024]{1,0:T(8,128)}), f32[8,128]{1,0:T(8,128)}) %reduce-scatter.14.cloned.1.call-update) | async-done | bytes 4112 | tf_op jit(solution)/shard_map/reduce_scatter | solution.py:82
  353.4 5.8 %all-reduce = f32[8,128]{1,0:T(8,128)S(1)} all-reduce(f32[8,128]{1,0:T(8,128)} %reduce-scatter.14.cloned.1.call-done), channel_id=7, replica_groups=mesh['dp'=4,'expert'=8] {'dp'}, use_global_device_ids=true, to_apply=%region_16.17.clone | all-reduce | flops 1024 | bytes 8192
  359.7 60.1 %reduce-scatter.8.cloned.1.call-done = bf16[128,512]{1,0:T(8,128)(2,1)} async-done(((bf16[1024,512]{1,0:T(8,128)(2,1)}), bf16[128,512]{1,0:T(8,128)(2,1)}) %reduce-scatter.8.cloned.1.call-update) | async-done | bytes 131088 | tf_op jit(solution)/shard_map/reduce_scatter | solution.py:66
  419.8 66.7 %reduce-scatter.12.cloned.1.call-done = bf16[128,512]{1,0:T(8,128)(2,1)} async-done(((bf16[1024,512]{1,0:T(8,128)(2,1)}), bf16[128,512]{1,0:T(8,128)(2,1)}) %reduce-scatter.12.cloned.1.call-update) | async-done | bytes 131088 | tf_op jit(solution)/shard_map/reduce_scatter | solution.py:78
  (83 shorter events, 11.8 us)
Async XLA Ops:
  7.2 45.8 %all-gather.5.cloned.1.call-start = ((), (), s32[]{:S(2)}) async-start(), calls=%async_computation.5 | async-start | bytes 1179648 | tf_op jit(solution)/shard_map/all_gather | solution.py:23
  7.9 86.2 %all-gather.9.cloned.1.call-start = ((), (), s32[]{:S(2)}) async-start(), calls=%async_computation.9 | async-start | bytes 1179648 | tf_op jit(solution)/shard_map/all_gather | solution.py:25
  8.6 157.1 %all-gather.7.cloned.1.call-start = ((), (), s32[]{:S(2)}) async-start(), calls=%async_computation.6 | async-start | bytes 5242880 | tf_op jit(solution)/shard_map/all_gather | solution.py:24
  53.0 126.9 %all-gather.11.cloned.1.call-start = ((), (), s32[]{:S(2)}) async-start(), calls=%async_computation.10 | async-start | bytes 5242880 | tf_op jit(solution)/shard_map/all_gather | solution.py:26
  94.1 155.5 %reduce-scatter.6.cloned.1.call-start = ((), (), s32[]{:S(2)}) async-start(), calls=%async_computation.7 | async-start | bytes 5242880 | tf_op jit(solution)/shard_map/reduce_scatter | solution.py:65
  158.9 5.6 %copy-start = (bf16[2,384,2048]{2,1,0:T(8,128)(2,1)S(1)}, bf16[2,384,2048]{2,1,0:T(8,128)(2,1)}, u32[]{:S(2)}) copy-start(bf16[2,384,2048]{2,1,0:T(8,128)(2,1)} %param.13) | copy-start | bytes 9437188
  165.8 7.1 %copy-start.1 = (bf16[1,384,2048]{2,1,0:T(8,128)(2,1)S(1)}, bf16[1,384,2048]{2,1,0:T(8,128)(2,1)}, u32[]{:S(2)}) copy-start(bf16[1,384,2048]{2,1,0:T(8,128)(2,1)} %constant_dynamic-slice_fusion.2) | copy-start | bytes 4718596
  172.9 3.6 copy-start.4
  173.0 3.6 copy-start.10
  173.0 4.5 copy-start.17
  179.9 7.9 %copy-start.9 = (f32[3,352,384]{2,1,0:T(8,128)}, f32[3,352,384]{2,1,0:T(8,128)S(1)}, u32[]{:S(2)}) copy-start(f32[3,352,384]{2,1,0:T(8,128)S(1)} %fusion.17) | copy-start | bytes 4866052
  179.9 7.9 %copy-start.7 = (f32[3,352,384]{2,1,0:T(8,128)S(1)}, f32[3,352,384]{2,1,0:T(8,128)}, u32[]{:S(2)}) copy-start(f32[3,352,384]{2,1,0:T(8,128)} %fusion.19) | copy-start | bytes 4866052
  179.9 7.9 %copy-start.13 = (bf16[1,384,2048]{2,1,0:T(8,128)(2,1)S(1)}, bf16[1,384,2048]{2,1,0:T(8,128)(2,1)}, u32[]{:S(2)}) copy-start(bf16[1,384,2048]{2,1,0:T(8,128)(2,1)} %constant_dynamic-slice_fusion) | copy-start | bytes 4718596
  179.9 7.9 %copy-start.16 = (bf16[2,384,2048]{2,1,0:T(8,128)(2,1)S(1)}, bf16[2,384,2048]{2,1,0:T(8,128)(2,1)}, u32[]{:S(2)}) copy-start(bf16[2,384,2048]{2,1,0:T(8,128)(2,1)} %param.15) | copy-start | bytes 9437188
  187.8 2.6 copy-start.3
  187.8 4.0 copy-start.8
  194.2 0.9 copy-start.5
  206.2 1.4 copy-start.2
  206.2 90.5 %reduce-scatter.10.cloned.1.call-start = ((), (), s32[]{:S(2)}) async-start(), calls=%async_computation.11 | async-start | bytes 5242880 | tf_op jit(solution)/shard_map/reduce_scatter | solution.py:77
  228.6 22.4 %copy-start.20 = (u32[32]{0:T(128)S(1)}, u32[32]{0:T(128)}, u32[]{:S(2)}) copy-start(u32[32]{0:T(128)} %constant.48) | copy-start | bytes 388
  228.7 124.7 %reduce-scatter.14.cloned.1.call-start = ((), (), s32[]{:S(2)}) async-start(), calls=%async_computation.13 | async-start | bytes 36864 | tf_op jit(solution)/shard_map/reduce_scatter | solution.py:82
  229.4 190.4 %reduce-scatter.8.cloned.1.call-start = ((), (), s32[]{:S(2)}) async-start(), calls=%async_computation.8 | async-start | bytes 1179648 | tf_op jit(solution)/shard_map/reduce_scatter | solution.py:66
  249.6 237.0 %reduce-scatter.12.cloned.1.call-start = ((), (), s32[]{:S(2)}) async-start(), calls=%async_computation.12 | async-start | bytes 1179648 | tf_op jit(solution)/shard_map/reduce_scatter | solution.py:78
  254.9 5.4 %copy-start.14 = (bf16[352,2048]{1,0:T(8,128)(2,1)}, bf16[352,2048]{1,0:T(8,128)(2,1)S(1)}, u32[]{:S(2)}) copy-start(bf16[352,2048]{1,0:T(8,128)(2,1)S(1)} %get-tuple-element.21) | copy-start | bytes 4325380
  254.9 5.4 %copy-start.15 = (bf16[352,2048]{1,0:T(8,128)(2,1)}, bf16[352,2048]{1,0:T(8,128)(2,1)S(1)}, u32[]{:S(2)}) copy-start(bf16[352,2048]{1,0:T(8,128)(2,1)S(1)} %get-tuple-element.22) | copy-start | bytes 4325380
  254.9 1.8 copy-start.6
  260.3 36.5 %copy-start.18 = (bf16[352,384]{1,0:T(8,128)(2,1)S(1)}, bf16[352,384]{1,0:T(8,128)(2,1)}, u32[]{:S(2)}) copy-start(bf16[352,384]{1,0:T(8,128)(2,1)} %get-tuple-element.44) | copy-start | bytes 811012
  260.3 36.5 %copy-start.19 = (bf16[352,384]{1,0:T(8,128)(2,1)S(1)}, bf16[352,384]{1,0:T(8,128)(2,1)}, u32[]{:S(2)}) copy-start(bf16[352,384]{1,0:T(8,128)(2,1)} %get-tuple-element.45) | copy-start | bytes 811012
  296.8 3.4 slice-start
  296.8 3.4 slice-start.1
  302.3 1.5 copy-start.12
  305.7 1.9 copy-start.11
Sparse Core Ops, SparseCore 0:
  10.1 42.8 all-gather.4
  55.1 38.8 all-gather.8
  95.6 33.2 all-gather.6
  130.3 34.4 all-gather.10
  206.3 43.2 reduce-scatter.5
  252.1 44.5 reduce-scatter.9
  299.9 53.4 reduce-scatter.13
  357.4 62.4 reduce-scatter.7
  424.2 62.3 reduce-scatter.11
